TPU v7x, 512 devices: a whole 4x4x16 slice. The times are simulated.
512 devices in a mesh: blk: 8 (over y, core), dp: 32 (over x_lo, z), mp: 2 (over x_hi).
Axes of the slice: x: 4 (x_hi: 2, x_lo: 2; x = x_hi * 2 + x_lo), y: 4, z: 16, core: 2. Of those that a mesh axis runs over, the one named last changes fastest.
Arguments:
- residual_tokens: bfloat16 [32, 8, 640, 1152], P('dp', 'blk'), may hold values from -20 to 20
- patch_tallies: int32 [32, 8], P('dp', 'blk'), may hold values from 106 to 640, as said below
- picture_assignment: int32 [32, 8, 640], P('dp', 'blk'), may hold values from 0 to 8, as said below
- normalizer_multiplier: float32 [1152], replicated, may hold values from 0.1 to 1.9
- expanding_matrix: bfloat16 [1152, 4304], P('dp', 'mp'), may hold values from -0.1875 to 0.1875
- contracting_matrix: bfloat16 [4304, 1152], P('mp', 'dp'), may hold values from -0.09375 to 0.09375
- sentence_vectors: bfloat16 [32, 64, 1152], P('dp', ('blk', 'mp')), may hold values from -20 to 20
- described_picture_number: int32 [32, 64], P('dp', ('blk', 'mp')), may hold values from 0 to 63
- similarity_multiplier: float32 [1], replicated, may hold values from 8 to 16
- additive_shift_term: float32 [1], replicated, may hold values from -4 to -1
Outputs:
- image_features: float32 [32, 64, 1152], P('dp', ('blk', 'mp'))
- image_grads: float32 [32, 64, 1152], P('dp', ('blk', 'mp'))
- text_grads: float32 [32, 64, 1152], P('dp', ('blk', 'mp'))
Inputs may be any that keep to these rules, and one draw needn't show every extreme that they name: `patch_tallies`: at least one pack is full. `picture_assignment`: along a pack the ids never fall; its first patch_tallies[g, b] rows hold 7 or 8 images numbered from 0, each covering one or more of those rows; the other rows hold 8.
All inputs are finite; a program needn't handle non-finite values.
Results may differ from a plain program's by a relative error of at most 0.015.
Values may be sent and summed in bfloat16 or wider, within the bound.
A program may use at most 64 MiB of HBM per device.

v0:
```python
import jax
import jax.numpy as jnp
from jax import lax
from jax.sharding import PartitionSpec as P

highest = lax.Precision.HIGHEST


def unit_rows(values):
    return (values * lax.rsqrt(jnp.sum(values * values, axis=1, keepdims=True) + 1e-06)).astype(
        jnp.bfloat16
    )


def pair_weights(image_rows, text_rows, signs, multiplier_coefficient, offset):
    logits = (
        multiplier_coefficient
        * jnp.einsum("pd,qd->pq", image_rows, text_rows, preferred_element_type=jnp.float32)
        + offset
    )
    return (multiplier_coefficient * -signs * jax.nn.sigmoid(-signs * logits)).astype(jnp.bfloat16)


def per_device(
    residual_tokens,
    patch_tallies,
    picture_assignment,
    normalizer_multiplier,
    expanding_matrix,
    contracting_matrix,
    sentence_vectors,
    described_picture_number,
    similarity_multiplier,
    additive_shift_term,
):
    pack_rows = residual_tokens[0, 0]
    count = patch_tallies[0, 0]
    slot_ids = picture_assignment[0, 0]
    rows_total = pack_rows.shape[0]
    pairs = sentence_vectors.shape[1]
    image_slots = pairs * lax.axis_size("mp")
    values = pack_rows.astype(jnp.float32)
    center = values - jnp.mean(values, axis=1, keepdims=True)
    spread = jnp.mean(center * center, axis=1, keepdims=True)
    normed = (center * lax.rsqrt(spread + 1e-06) * normalizer_multiplier).astype(jnp.bfloat16)
    up_full = lax.all_gather(expanding_matrix, "dp", axis=0, tiled=True)
    preact = jnp.dot(normed, up_full, preferred_element_type=jnp.float32)
    hidden = jax.nn.gelu(preact, approximate=True).astype(jnp.bfloat16)
    slots = lax.broadcasted_iota(jnp.int32, (image_slots, rows_total), 0)
    positions = lax.broadcasted_iota(jnp.int32, (image_slots, rows_total), 1)
    member = ((slot_ids[None, :] == slots) & (positions < count)).astype(jnp.bfloat16)
    sizes = jnp.maximum(jnp.sum(member.astype(jnp.float32), axis=1, keepdims=True), 1.0)
    layer_out = jnp.dot(
        hidden,
        lax.all_gather(contracting_matrix, "dp", axis=1, tiled=True),
        preferred_element_type=jnp.float32,
    )
    pooled = jnp.dot(member.astype(jnp.float32), layer_out, precision=highest) / sizes
    pooled_mine = lax.psum_scatter(pooled, "mp", scatter_dimension=0, tiled=True)
    lower_slot = lax.axis_index("mp") * pairs
    member_mine = lax.dynamic_slice_in_dim(member, lower_slot, pairs, 0)
    sizes_mine = lax.dynamic_slice_in_dim(sizes, lower_slot, pairs, 0)
    features = (
        jnp.dot(member_mine, pack_rows, preferred_element_type=jnp.float32) / sizes_mine
        + pooled_mine
    )
    multiplier_coefficient = similarity_multiplier[0]
    offset = additive_shift_term[0]
    image_unit = unit_rows(features)
    text_unit = unit_rows(sentence_vectors[0].astype(jnp.float32))
    cycle_index = lax.axis_index(("blk", "mp"))
    group_ids = lax.all_gather(described_picture_number[0], ("blk", "mp"), axis=0, tiled=True)
    own_images = cycle_index * pairs + lax.iota(jnp.int32, pairs)
    piece = lax.all_gather(text_unit, ("blk", "mp"), axis=0, tiled=True)
    signs = jnp.where(group_ids[None, :] == own_images[:, None], 1.0, -1.0).astype(jnp.float32)
    weights = pair_weights(image_unit, piece, signs, multiplier_coefficient, offset)
    image_sum = jnp.dot(weights, piece, preferred_element_type=jnp.float32)
    text_term = jnp.einsum("pq,pd->qd", weights, image_unit, preferred_element_type=jnp.float32)
    text_grads = lax.psum_scatter(text_term, ("blk", "mp"), scatter_dimension=0, tiled=True)
    return (features[None], image_sum[None], text_grads[None])


def solution(mesh):
    in_specs = (
        P("dp", "blk", None, None),
        P("dp", "blk"),
        P("dp", "blk", None),
        P(),
        P("dp", "mp"),
        P("mp", "dp"),
        P("dp", ("blk", "mp"), None),
        P("dp", ("blk", "mp")),
        P(),
        P(),
    )
    out_specs = (
        P("dp", ("blk", "mp"), None),
        P("dp", ("blk", "mp"), None),
        P("dp", ("blk", "mp"), None),
    )
    return jax.shard_map(
        per_device, mesh=mesh, in_specs=in_specs, out_specs=out_specs, check_vma=False
    )
```

profile of v0, /device:TPU:1, one launch (start us, length us, event | category | flops | bytes accessed | tf_op | source)
XLA Modules:
  0.0 487.9 jit_solution(5186446927876231588)
XLA Ops:
  7.2 0.0 copy-start
  7.2 0.0 all-gather.7.cloned.1.call-start
  7.2 0.7 all-gather.7.cloned.1.call-update
  7.9 0.0 all-gather.9.cloned.1.call-start
  8.0 0.7 all-gather.9.cloned.1.call-update
  8.7 0.0 all-reduce.5.cloned.1.call-start
  10.7 0.7 reduce
  11.4 0.8 fusion.40
  12.2 0.8 fusion.43
  13.0 40.7 %all-gather.3 = bf16[16,4,1152]{2,1,0:T(4,128)(2,1)S(1)} all-gather(bf16[1,4,1152]{2,1,0:T(4,128)(2,1)S(1)} %fusion.43), channel_id=1, replica_groups=mesh['blk'=8,'dp'=32,'mp'=2] {'blk','mp'}, dimensions={0}, use_global_device_ids=true | all-gather | bytes 156672 | tf_op jit(solution)/shard_map/all_gather | solution.py:74
  53.8 1.3 dynamic-slice.5
  55.7 1.4 fusion.51
  57.7 0.1 convert_reduce_fusion.1
  57.8 0.1 dynamic-slice.3
  57.9 0.7 bitcast_dynamic-update-slice_fusion
  58.7 10.0 %all-reduce = s32[64]{0:T(128)S(1)} all-reduce(s32[64]{0:T(128)S(1)} %bitcast_dynamic-update-slice_fusion), channel_id=2, replica_groups=mesh['blk'=8,'dp'=32,'mp'=2] {'blk','mp'}, use_global_device_ids=true, to_apply=%add | all-reduce | flops 64 | bytes 512
  68.7 1.6 convert_reduce_fusion
  70.3 0.0 copy-done
  70.3 0.5 fusion.10
  70.9 66.9 %all-gather.7.cloned.1.call-done = bf16[32,36,2152]{2,1,0:T(8,128)(2,1)} async-done(((bf16[1,36,2152]{2,1,0:T(8,128)(2,1)}), bf16[32,36,2152]{2,1,0:T(8,128)(2,1)}) %all-gather.7.cloned.1.call-update) | async-done | bytes 4958224 | tf_op jit(solution)/shard_map/all_gather | solution.py:46
  137.8 7.9 %reshape.57 = bf16[1152,2152]{1,0:T(8,128)(2,1)} reshape(bf16[32,36,2152]{2,1,0:T(8,128)(2,1)} %all-gather.7.cloned.1.call-done) | data formatting | bytes 9916416
  145.7 0.0 copy-start.2
  145.7 129.6 %all-gather.9.cloned.1.call-done = bf16[32,36,2152]{2,1,0:T(8,128)(2,1)} async-done(((bf16[1,36,2152]{2,1,0:T(8,128)(2,1)}), bf16[32,36,2152]{2,1,0:T(8,128)(2,1)}) %all-gather.9.cloned.1.call-update) | async-done | bytes 4958224 | tf_op jit(solution)/shard_map/all_gather | solution.py:55
  275.3 7.9 %reshape.59 = bf16[1152,2152]{1,0:T(8,128)(2,1)} reshape(bf16[32,36,2152]{2,1,0:T(8,128)(2,1)} %all-gather.9.cloned.1.call-done) | data formatting | bytes 9916416
  283.2 0.0 copy-done.2
  283.2 15.6 %fusion.13 = f32[640,1152]{1,0:T(8,128)} fusion(bf16[1152,2152]{1,0:T(8,128)(2,1)} %reshape.59, bf16[1152,2152]{1,0:T(8,128)(2,1)} %reshape.57, bf16[1,1,640,1152]{3,2,1,0:T(8,128)(2,1)S(1)} %copy-done, f32[1152]{0:T(1024)S(1)} %copy-done.2, f32[640]{0:T(1024)S(1)} %add_rsqrt_fusion, f32[640]{0:T(1024)S(1)} %broadcast_multiply_fusion), kind=kOutput, calls=%fused_computation.16 | convolution fusion | flops 6362588160 | bytes 14349824 | tf_op jit(solution)/shard_map/dot_general | solution.py:53
  298.7 2.9 convolution_divide_fusion
  301.6 9.1 %all-reduce.1 = f32[8,1152]{1,0:T(8,128)S(1)} all-reduce(f32[8,1152]{1,0:T(8,128)S(1)} %convolution_divide_fusion), channel_id=3, replica_groups=mesh['blk'=8,'dp'=32,'mp'=2] {'mp'}, use_global_device_ids=true, to_apply=%region_3.0.clone | all-reduce | flops 9216 | bytes 73728
  310.8 0.4 multiply_reduce_fusion
  311.2 0.0 copy-start.1
  311.2 0.2 fusion.38
  311.4 1.0 fusion.49
  312.5 0.0 all-reduce.5.cloned.1.call-update
  313.1 0.7 convolution_bitcast_fusion
  313.9 166.1 %all-reduce.5.cloned.1.call-done = f32[64,1152]{1,0:T(8,128)} async-done(((f32[64,1152]{1,0:T(8,128)}), f32[64,1152]{1,0:T(8,128)}) %all-reduce.5.cloned.1.call-update) | async-done | bytes 294928
  480.0 1.4 dynamic-slice_bitcast_fusion
  481.4 0.0 copy-done.1
  (9 shorter events, 0.1 us)
Async XLA Ops:
  7.2 63.2 %copy-start = (bf16[1,1,640,1152]{3,2,1,0:T(8,128)(2,1)S(1)}, bf16[1,1,640,1152]{3,2,1,0:T(8,128)(2,1)}, u32[]{:S(2)}) copy-start(bf16[1,1,640,1152]{3,2,1,0:T(8,128)(2,1)} %param.10) | copy-start | bytes 4423684
  7.2 130.6 %all-gather.7.cloned.1.call-start = ((), (), s32[]{:S(2)}) async-start(), calls=%async_computation | async-start | bytes 5744640 | tf_op jit(solution)/shard_map/all_gather | solution.py:46
  7.9 267.4 %all-gather.9.cloned.1.call-start = ((), (), s32[]{:S(2)}) async-start(), calls=%async_computation.1 | async-start | bytes 5744640 | tf_op jit(solution)/shard_map/all_gather | solution.py:55
  8.7 471.3 %all-reduce.5.cloned.1.call-start = ((), (), s32[]{:S(2)}) async-start(), calls=%async_computation.2 | async-start | bytes 589824
  145.7 137.5 %copy-start.2 = (f32[1152]{0:T(1024)S(1)}, f32[1152]{0:T(1024)}, u32[]{:S(2)}) copy-start(f32[1152]{0:T(1024)} %param.13) | copy-start | bytes 13828
  311.2 170.2 %copy-start.1 = (f32[4,1152]{1,0:T(4,128)}, f32[4,1152]{1,0:T(4,128)S(1)}, u32[]{:S(2)}) copy-start(f32[4,1152]{1,0:T(4,128)S(1)} %get-tuple-element.8) | copy-start | bytes 55300
Sparse Core Ops, SparseCore 0:
  10.1 127.6 all-gather.6
  139.8 135.3 all-gather.8
  312.6 167.3 all-reduce.4
where the time goes:
time: 489 us; the launch traced here: 488 us
  waiting for transfers between devices  364 us (74%)
  blocking collectives  59.9 us (12%)
  matrix products  20.8 us (4%)
  local copies, waits for them, and re-layouts  20.7 us (4%)
  between operations  17.7 us (4%)
    unnamed x4, waiting for transfers between devices  168 us
    all_gather x1, waiting for transfers between devices, per_device(): lax.all_gather(contracting_matrix, 'dp', axis=1, tiled=True)  130 us
    all_gather x1, waiting for transfers between devices, per_device(): up_full = lax.all_gather(expanding_matrix, 'dp', axis=0, tiled=True)  66.9 us
    all_gather x1, blocking collectives, per_device(): piece = lax.all_gather(text_unit, ('blk', 'mp'), axis=0, tiled=True)  40.7 us
    unnamed x13, local copies, waits for them, and re-layouts  19.2 us
    unnamed x2, blocking collectives  19.2 us
    dot_general x1, matrix products, per_device(): jnp.dot(hidden, lax.all_gather(contracting_matrix, 'dp', axis=1, tiled=Tr...  15.6 us
  transfers between devices with their start and end apart: 3, of which 3 were waited for; matrix products, arithmetic and copies ran while one was open for 3% of the time, Pallas kernels for 0%

commit v1 on v0

v1 whole, which is shorter than its diff:
```python
import numpy as np
import jax
import jax.numpy as jnp
from jax import lax
from jax.experimental import pallas as pl
from jax.experimental.pallas import tpu as pltpu
from jax.sharding import PartitionSpec as P

MESH = pl.DeviceIdType.MESH
F32 = jnp.float32
BF16 = jnp.bfloat16
D = 1152
ROWS = 640
PIECE = 36
SET = 4 * PIECE
LANES = 128
HOPS = (1, -1, 2)
NT = (((1,), (1,)), ((), ()))


def column_origin():
    out = np.zeros((1, D), np.int32)
    for x in range(2):
        for z in range(16):
            k, rho = z // 4, z % 4
            at = SET * (rho * 2 + x) + PIECE * k
            out[0, at : at + PIECE] = PIECE * (x * 16 + z) + np.arange(PIECE)
    return out


def gelu(u):
    return 0.5 * u * (1.0 + jnp.tanh(0.7978845608028654 * (u + 0.044715 * (u * u * u))))


def two_bands(values):
    return jnp.concatenate([values[:, :640], values[:, 640:]], axis=0).astype(BF16)


def kernel(
    x_ref,
    count_ref,
    slot_ref,
    gain_ref,
    w1_ref,
    w2_ref,
    text_ref,
    ids_ref,
    mult_ref,
    shift_ref,
    origin_ref,
    features_out,
    image_out,
    text_out,
    pieces,
    w1,
    w2,
    perm,
    normed,
    member,
    texts,
    units,
    pooled,
    pooled_in,
    window,
    partial,
    returned,
    send_sem,
    recv_sem,
):
    blk, dp, mp = lax.axis_index("blk"), lax.axis_index("dp"), lax.axis_index("mp")
    y, c = lax.div(blk, 2), lax.rem(blk, 2)
    xl, z = lax.div(dp, 16), lax.rem(dp, 16)
    rho, k0 = lax.rem(z, 4), lax.div(z, 4)

    def dev(dy=0, dz=0, yy=None, cc=None, xx=None, mm=None):
        yy = lax.rem(y + dy + 8, 4) if yy is None else yy
        zz = lax.rem(z + dz + 32, 16)
        cc = c if cc is None else cc
        xx = xl if xx is None else xx
        mm = mp if mm is None else mm
        return {"blk": yy * 2 + cc, "dp": xx * 16 + zz, "mp": mm}

    def u_dev(off):
        return dev(dy=off * c, dz=off * (1 - c))

    def v_dev(off):
        return dev(dy=off * (1 - c), dz=off * c)

    started = []
    channels = [0]

    def send(src, dst, where, when=None):
        ch = channels[0]
        channels[0] += 1
        copy = pltpu.make_async_remote_copy(
            src_ref=src,
            dst_ref=dst,
            send_sem=send_sem.at[ch],
            recv_sem=recv_sem.at[ch],
            device_id=where,
            device_id_type=MESH,
        )
        if when is None:
            copy.start()
        else:
            pl.when(when)(copy.start)
        started.append((copy, when))
        return copy

    barrier = pltpu.get_barrier_semaphore()
    peers = [dev(dz=4), dev(dz=8), dev(dz=12)]
    for dx in (0, 1):
        for dz in (-2, -1, 0, 1, 2):
            for dm in (0, 1):
                if (dx, dz, dm) != (0, 0, 0):
                    peers.append(dev(dz=dz, xx=lax.rem(xl + dx, 2), mm=lax.rem(mp + dm, 2)))
    for dy in range(4):
        for dc in (0, 1):
            for dm in (0, 1):
                if (dy, dc) != (0, 0):
                    peers.append(dev(dy=dy, cc=lax.rem(c + dc, 2), mm=lax.rem(mp + dm, 2)))
    for peer in peers:
        pl.semaphore_signal(barrier, inc=1, device_id=peer, device_id_type=MESH)

    def two_tiles(a, b):
        both = [a.astype(F32), b.astype(F32), jnp.zeros((8, LANES), F32)]
        return jnp.concatenate(both, axis=0).astype(BF16)

    def tile_of(ref, index):
        return ref[:, pl.ds(pl.multiple_of(index * LANES, LANES), LANES)]

    def odd_tile(ref):
        part = ref[:, 2048:2152].astype(F32)
        return jnp.concatenate([part, jnp.zeros((PIECE, 24), F32)], axis=1)

    pieces[0, k0] = two_tiles(tile_of(w1_ref, c * 8 + y), tile_of(w1_ref, c * 8 + 4 + y))
    pieces[1, k0] = two_tiles(odd_tile(w1_ref), odd_tile(w2_ref))
    pieces[2, k0] = two_tiles(tile_of(w2_ref, c * 8 + y), tile_of(w2_ref, c * 8 + 4 + y))
    pl.semaphore_wait(barrier, len(peers))
    is_even = c == 0
    first = [
        [send(pieces.at[j, k0], pieces.at[j, k0], dev(dz=dz), is_even if j == 1 else None) for dz in (8, 4, 12)]
        for j in range(3)
    ]

    text = text_ref[...].astype(F32)
    text = text * lax.rsqrt(jnp.sum(text * text, axis=1, keepdims=True) + 1e-06)
    diagonal = lax.broadcasted_iota(jnp.int32, (4, 4), 0) == lax.broadcasted_iota(jnp.int32, (4, 4), 1)
    ids = jnp.sum(jnp.where(diagonal, jnp.broadcast_to(ids_ref[...], (4, 4)), 0).astype(F32), axis=1, keepdims=True)
    own_text = jnp.concatenate([text, jnp.broadcast_to(ids, (4, LANES))], axis=1)
    own_text = jnp.concatenate([own_text, jnp.zeros((4, D + LANES), F32)], axis=0)
    own_slot = blk * 2 + mp
    texts[own_slot] = two_bands(own_text)
    text_sends = []
    for dy in range(4):
        for dc in (0, 1):
            for dm in (0, 1):
                if (dy, dc, dm) != (0, 0, 0):
                    where = dev(dy=dy, cc=lax.rem(c + dc, 2), mm=lax.rem(mp + dm, 2))
                    text_sends.append(send(texts.at[own_slot], texts.at[own_slot], where))
    positions = lax.broadcasted_iota(jnp.int32, (8, ROWS), 1)
    slots = lax.broadcasted_iota(jnp.int32, (8, ROWS), 0)
    is_member = (jnp.broadcast_to(slot_ref[...], (8, ROWS)) == slots) & (positions < count_ref[0])
    own_member = jnp.where(is_member, 1.0, 0.0).astype(F32)
    member[c] = own_member
    core = dev(cc=1 - c)
    member_send = send(member.at[c], member.at[c], core)
    own_sizes = jnp.maximum(jnp.sum(own_member, axis=1, keepdims=True), 1.0)

    chunk = 128

    def perm_step(i, _):
        rows = pl.ds(pl.multiple_of(i * chunk, chunk), chunk)
        origin = lax.broadcasted_iota(jnp.int32, (chunk, D), 0) + i * chunk
        perm[rows, :] = jnp.where(origin == origin_ref[...], 1.0, 0.0).astype(BF16)
        return 0

    lax.fori_loop(0, D // chunk, perm_step, 0)

    def norm_step(i, _):
        rows = pl.ds(pl.multiple_of(i * chunk, chunk), chunk)
        values = x_ref[rows, :].astype(F32)
        center = values - jnp.mean(values, axis=1, keepdims=True)
        spread = jnp.mean(center * center, axis=1, keepdims=True)
        scaled = (center * lax.rsqrt(spread + 1e-06) * gain_ref[...]).astype(BF16)
        normed[c, rows, :] = jnp.dot(scaled, perm[...], preferred_element_type=F32).astype(BF16)
        return 0

    lax.fori_loop(0, ROWS // chunk, norm_step, 0)
    normed_send = send(normed.at[c], normed.at[c], core)
    patch_mean = jnp.dot(own_member.astype(BF16), x_ref[...], preferred_element_type=F32) / own_sizes

    def rows_of(r, x=None):
        if x is None:
            return pl.ds(pl.multiple_of(r * 2 * SET, 16), 2 * SET)
        return pl.ds(pl.multiple_of((r * 2 + x) * SET, 16), SET)

    def place(a, o=0):
        yy = lax.rem(y + 8 - a * c - o * (1 - c), 4)
        rr = lax.rem(rho + 8 - a * (1 - c) - o * c, 4)
        return yy, rr

    def block(tile, rows):
        return w1.at[tile, rows]

    def push(ref, where, when=None):
        return send(ref, ref, where, when)

    def stacked(j, t):
        parts = [pieces[j, k].astype(F32)[PIECE * t : PIECE * (t + 1)] for k in range(4)]
        return jnp.concatenate(parts, axis=0).astype(BF16)

    partner = dev(xx=1 - xl)
    for copy in first[0]:
        copy.wait_recv()
    for t in range(2):
        w1[t * 4 + y, rows_of(rho, xl), :] = stacked(0, t)
    mine = block(y, rows_of(rho, xl))
    own1 = block(4 + y, rows_of(rho, xl))
    a1 = push(mine, partner)
    b1 = [push(own1, u_dev(o)) for o in HOPS]
    b2 = {(0, o): push(own1, v_dev(o)) for o in HOPS}
    b3 = [push(own1, partner)]

    a1.wait_recv()
    pair = block(y, rows_of(rho))
    a2 = [push(pair, u_dev(o)) for o in HOPS]
    a3 = [push(pair, v_dev(o)) for o in HOPS]

    for copy in first[1]:
        pl.when(is_even)(copy.wait_recv)

    @pl.when(is_even)
    def _():
        w1[8, rows_of(rho, xl), :] = stacked(1, 0)
        w2[16] = stacked(1, 1)

    odd1 = push(block(8, rows_of(rho, xl)), partner, is_even)
    for copy in first[2]:
        copy.wait_recv()
    for t in range(2):
        w2[c * 8 + y * 2 + t] = stacked(2, t)
    own2 = w2.at[pl.ds(c * 8 + y * 2, 2)]
    w2_sends = [push(own2, dev(dy=dy)) for dy in (1, 3, 2)]
    pl.when(is_even)(odd1.wait_recv)
    odd2 = [push(block(8, rows_of(rho)), dev(dz=o), is_even) for o in HOPS]

    for a, copy in zip(HOPS, b1):
        copy.wait_recv()
        yy, rr = place(a)
        ref = block(4 + yy, rows_of(rr, xl))
        for o in HOPS:
            b2[a, o] = push(ref, v_dev(o))
        b3.append(push(ref, partner))
    for a, copy in zip(HOPS, a2):
        copy.wait_recv()
        yy, rr = place(a)
        ref = block(yy, rows_of(rr))
        for o in HOPS:
            a3.append(push(ref, v_dev(o)))
    for (a, o), copy in list(b2.items()):
        copy.wait_recv()
        yy, rr = place(a, o)
        b3.append(push(block(4 + yy, rows_of(rr, xl)), partner))

    member_send.wait_recv()
    normed_send.wait_recv()

    def tile_work(first_tile, tiles):
        if tiles == 2:
            weights = jnp.concatenate([w1[first_tile], w1[first_tile + 1]], axis=1)
        else:
            weights = w1[first_tile]
        for q in range(2):
            hidden = gelu(jnp.dot(normed[q], weights, preferred_element_type=F32)).astype(BF16)
            sums = jnp.dot(member[q].astype(BF16), hidden, preferred_element_type=F32)
            sizes = jnp.maximum(jnp.sum(member[q], axis=1, keepdims=True), 1.0)
            for t in range(tiles):
                pooled[q, first_tile + t] = sums[:, LANES * t : LANES * (t + 1)] / sizes

    def pair_step(i, _):
        tile_work(2 * i, 2)
        return 0

    for copy in a3:
        copy.wait_recv()
    lax.fori_loop(0, 2, pair_step, 0)
    for copy in w2_sends:
        copy.wait_recv()
    half = w2.at[pl.ds(c * 8, 8)]
    w2_core = push(half, core)
    w2_odd = send(w2.at[16], w2.at[16], core, is_even)
    for copy in odd2:
        pl.when(is_even)(copy.wait_recv)
    pl.when(is_even)(lambda: tile_work(8, 1))

    @pl.when(c == 1)
    def _():
        pooled[:, 8] = jnp.zeros((2, 8, LANES), F32)

    for copy in b3:
        copy.wait_recv()
    lax.fori_loop(2, 4, pair_step, 0)

    pooled_send = send(pooled.at[1 - c], pooled_in, core)
    pooled_send.wait_recv()
    own = jnp.concatenate([pooled[c, t] for t in range(9)], axis=1)
    other = jnp.concatenate([pooled_in[t] for t in range(9)], axis=1)
    low = jnp.where(is_even, own, other)
    high = jnp.where(is_even, other, own)
    own_window = xl * 4
    window[own_window] = jnp.concatenate([low, high], axis=0).astype(BF16)
    window_sends = []
    for n, o in enumerate((0,) + HOPS):
        for dx in (0, 1):
            if (o, dx) == (0, 0):
                continue
            where = dev(dz=o, xx=lax.rem(xl + dx, 2))
            window_sends.append(send(window.at[own_window], window.at[own_window + n], where))
    w2_core.wait_recv()
    pl.when(c == 1)(w2_odd.wait_recv)
    order = [yy * 2 + t for t in range(2) for yy in range(4)]
    low2 = jnp.concatenate([w2[n] for n in order] + [w2[16]], axis=1)
    high2 = jnp.concatenate([w2[8 + n] for n in order], axis=1)
    for copy in window_sends:
        copy.wait_recv()
    gathered = window[...].astype(F32)
    low1 = gathered[:, :8].reshape(64, D).astype(BF16)
    high1 = gathered[:, 8:, :1024].reshape(64, 1024).astype(BF16)
    result = lax.dot_general(low1, low2, NT, preferred_element_type=F32)
    result = result + lax.dot_general(high1, high2, NT, preferred_element_type=F32)
    partial[...] = jnp.concatenate([result, jnp.zeros((64, 256 - SET), F32)], axis=1)
    my_set = mp * 8 + rho * 2 + xl
    returned_sends = []
    for n, o in enumerate((0,) + HOPS):
        for dx in (0, 1):
            xx = lax.rem(xl + dx, 2)
            rows = partial.at[pl.ds(pl.multiple_of((xx * 4 + n) * 8, 8), 8)]
            for dm in (0, 1):
                if (o, dx, dm) == (0, 0, 0):
                    continue
                where = dev(dz=-o, xx=xx, mm=lax.rem(mp + dm, 2))
                returned_sends.append(send(rows, returned.at[my_set], where))
    returned[my_set] = partial[pl.ds(pl.multiple_of(xl * 32, 8), 8), :]
    for copy in returned_sends:
        copy.wait_recv()
    sums = [returned[n] + returned[8 + n] for n in range(8)]
    columns = []
    for x in range(2):
        for zz in range(16):
            k, r = zz // 4, zz % 4
            columns.append(sums[r * 2 + x][:, PIECE * k : PIECE * (k + 1)])
    features = jnp.concatenate(columns, axis=1) + patch_mean
    features_out[...] = jnp.where(mp == 0, features[:4], features[4:])

    image_unit = features * lax.rsqrt(jnp.sum(features * features, axis=1, keepdims=True) + 1e-06)
    units[blk] = two_bands(jnp.concatenate([image_unit, jnp.zeros((8, LANES), F32)], axis=1))
    unit_sends = []
    for dy in range(4):
        for dc in (0, 1):
            if (dy, dc) != (0, 0):
                where = dev(dy=dy, cc=lax.rem(c + dc, 2))
                unit_sends.append(send(units.at[blk], units.at[blk], where))
    for copy in text_sends:
        copy.wait_recv()
    mult, shift = mult_ref[0], shift_ref[0]

    def weights_of(dots, same):
        signs = jnp.where(same, 1.0, -1.0).astype(F32)
        logits = mult * dots + shift
        return (mult * -signs * jax.nn.sigmoid(-signs * logits)).astype(BF16)

    captions = texts[...].astype(F32)
    all_text = jnp.concatenate([captions[:, :8], captions[:, 8:]], axis=2).reshape(128, D + LANES)
    id_column = all_text[:, D : D + 1]
    all_text = all_text[:, :D].astype(BF16)
    square = (128, 128)
    eye = lax.broadcasted_iota(jnp.int32, square, 0) == lax.broadcasted_iota(jnp.int32, square, 1)
    id_rows = jnp.dot(
        jnp.ones((8, 128), BF16), jnp.where(eye, id_column, 0.0).astype(BF16), preferred_element_type=F32
    )
    own_images = (lax.broadcasted_iota(jnp.int32, (8, 128), 0) + blk * 8).astype(F32)
    dots = lax.dot_general(image_unit.astype(BF16), all_text, NT, preferred_element_type=F32)
    image_weights = weights_of(dots, id_rows == own_images)
    image_grads = jnp.dot(image_weights, all_text, preferred_element_type=F32)
    image_out[...] = jnp.where(mp == 0, image_grads[:4], image_grads[4:])
    for copy in unit_sends:
        copy.wait_recv()
    bands = units[...].astype(F32)
    all_units = jnp.concatenate([bands[:, :8], bands[:, 8:, :512]], axis=2).reshape(64, D).astype(BF16)
    dots = lax.dot_general(own_text[:, :D].astype(BF16), all_units, NT, preferred_element_type=F32)
    image_ids = lax.broadcasted_iota(jnp.int32, (8, 64), 1).astype(F32)
    text_weights = weights_of(dots, own_text[:, D : D + 1] == image_ids)
    text_out[...] = jnp.dot(text_weights, all_units, preferred_element_type=F32)[:4]

    for copy, when in started:
        if when is None:
            copy.wait_send()
        else:
            pl.when(when)(copy.wait_send)


CHANNELS = 136


def per_device(x, tallies, slots, gain, w1, w2, texts, ids, mult, shift):
    vmem = pl.BlockSpec(memory_space=pltpu.VMEM)
    smem = pl.BlockSpec(memory_space=pltpu.SMEM)
    out = jax.ShapeDtypeStruct((4, D), F32)
    results = pl.pallas_call(
        kernel,
        out_shape=(out, out, out),
        in_specs=[vmem, smem, vmem, vmem, vmem, vmem, vmem, vmem, smem, smem, vmem],
        out_specs=(vmem, vmem, vmem),
        scratch_shapes=[
            pltpu.VMEM((3, 4, 80, LANES), BF16),
            pltpu.VMEM((9, D, LANES), BF16),
            pltpu.VMEM((17, SET, LANES), BF16),
            pltpu.VMEM((D, D), BF16),
            pltpu.VMEM((2, ROWS, D), BF16),
            pltpu.VMEM((2, 8, ROWS), F32),
            pltpu.VMEM((16, 16, 640), BF16),
            pltpu.VMEM((8, 16, 640), BF16),
            pltpu.VMEM((2, 9, 8, LANES), F32),
            pltpu.VMEM((9, 8, LANES), F32),
            pltpu.VMEM((8, 16, D), BF16),
            pltpu.VMEM((64, 256), F32),
            pltpu.VMEM((16, 8, 256), F32),
            pltpu.SemaphoreType.DMA((CHANNELS,)),
            pltpu.SemaphoreType.DMA((CHANNELS,)),
        ],
        compiler_params=pltpu.CompilerParams(
            collective_id=0, has_side_effects=True, vmem_limit_bytes=48 << 20
        ),
        name="siglip_step",
    )(
        x[0, 0],
        tallies[0],
        slots[0],
        gain[None],
        w1,
        w2.T,
        texts[0],
        ids,
        mult,
        shift,
        jnp.asarray(column_origin()),
    )
    return tuple(r[None] for r in results)


def solution(mesh):
    in_specs = (
        P("dp", "blk", None, None),
        P("dp", "blk"),
        P("dp", "blk", None),
        P(),
        P("dp", "mp"),
        P("mp", "dp"),
        P("dp", ("blk", "mp"), None),
        P("dp", ("blk", "mp")),
        P(),
        P(),
    )
    out_specs = (P("dp", ("blk", "mp"), None),) * 3
    return jax.shard_map(per_device, mesh=mesh, in_specs=in_specs, out_specs=out_specs, check_vma=False)
```

time: 489 us -> 88.6 us (0.18)
  waiting for transfers between devices: 364 us -> 0 us
  Pallas kernels: 0 us -> 77.2 us
  blocking collectives: 59.9 us -> 0 us
  matrix products: 20.8 us -> 0 us
  between operations: 17.7 us -> 2.59 us
  local copies, waits for them, and re-layouts: 20.7 us -> 8.45 us
    all_gather x2 -> x0, waiting for transfers between devices: 197 us -> none  [the longest x1 130 us: per_device(): lax.all_gather(contracting_matrix, 'dp', axis=1, tiled=True)]
    unnamed x4 -> x0, waiting for transfers between devices: 168 us -> none
    pallas_call x0 -> x1, Pallas kernels: none -> 77.2 us  [per_device(): pl.pallas_call(kernel, out_shape=(out, out, out), in_specs=[vmem, smem, v...]
    all_gather x1 -> x0, blocking collectives: 40.7 us -> none  [per_device(): piece = lax.all_gather(text_unit, ('blk', 'mp'), axis=0, tiled=True)]
    dot_general x6 -> x0, matrix products: 20.8 us -> none  [the longest x1 15.6 us: per_device(): jnp.dot(hidden, lax.all_gather(contracting_matrix, 'dp', axis=1, tiled=Tr...]
    unnamed x2 -> x0, blocking collectives: 19.2 us -> none
    unnamed x13 -> x17, local copies, waits for them, and re-layouts: 19.2 us -> 7.75 us
  transfers between devices with their start and end apart: 3 -> 0, of which waited for: 3 -> 0; matrix products, arithmetic and copies ran while one was open for 3% -> 0% of each run, Pallas kernels for 0% -> 0%
where the time goes in v1:
time: 88.6 us; the launch traced here: 88.2 us
  Pallas kernels  77.2 us (87%)
  local copies, waits for them, and re-layouts  8.45 us (10%)
  between operations  2.59 us (3%)
    pallas_call x1, Pallas kernels, per_device(): pl.pallas_call(kernel, out_shape=(out, out, out), in_specs=[vmem, smem, v...  77.2 us
    unnamed x17, local copies, waits for them, and re-layouts  7.75 us

profile of v1, /device:TPU:1, one launch (start us, length us, event | category | flops | bytes accessed | tf_op | source)
XLA Modules:
  0.0 88.2 jit_solution(2444331713222673085)
XLA Ops:
  2.6 0.7 broadcast_in_dim.12.gain_ref
  3.3 0.0 copy-start
  3.3 1.4 %copy-done = bf16[1,1,640,1152]{3,2,1,0:T(8,128)(2,1)S(1)} copy-done((bf16[1,1,640,1152]{3,2,1,0:T(8,128)(2,1)S(1)}, bf16[1,1,640,1152]{3,2,1,0:T(8,128)(2,1)}, u32[]{:S(2)}) %copy-start) | copy-done | bytes 1474584
  4.6 0.0 copy-start.1
  4.6 0.9 %copy-done.1 = bf16[36,2152]{1,0:T(8,128)(2,1)S(1)} copy-done((bf16[36,2152]{1,0:T(8,128)(2,1)S(1)}, bf16[36,2152]{1,0:T(8,128)(2,1)}, u32[]{:S(2)}) %copy-start.1) | copy-done | bytes 154968
  5.6 0.0 copy-start.2
  5.6 0.9 %copy-done.2 = bf16[2152,36]{0,1:T(8,128)(2,1)S(1)} copy-done((bf16[2152,36]{0,1:T(8,128)(2,1)S(1)}, bf16[2152,36]{0,1:T(8,128)(2,1)}, u32[]{:S(2)}) %copy-start.2) | copy-done | bytes 154968
  6.5 0.0 copy-start.3
  6.5 0.7 copy-done.3
  7.2 0.0 copy-start.4
  7.2 0.7 copy-done.4
  7.9 0.0 copy-start.5
  7.9 0.7 copy-done.5
  8.6 0.0 copy-start.6
  8.6 0.7 copy-done.6
  9.2 77.2 %siglip_step.1 = (f32[4,1152]{1,0:T(4,128)S(1)}, f32[4,1152]{1,0:T(4,128)S(1)}, f32[4,1152]{1,0:T(4,128)S(1)}) custom-call(bf16[640,1152]{1,0:T(8,128)(2,1)S(1)} %bitcast.9, s32[1]{0:T(128)} %bitcast.8.count_ref, s32[1,640]{1,0:T(1,128)S(1)} %bitcast.15, f32[1,1152]{1,0:T(1,128)S(1)} %broadcast_in_dim.12.gain_ref, bf16[36,2152]{1,0:T(8,128)(2,1)S(1)} %copy-done.1, ...), custom_call_target="tpu_custom_call" | custom-call | tf_op jit(solution)/shard_map/siglip_step/pallas_call | solution.py:410
  86.4 0.6 copy.20
  87.0 0.6 copy.21
  87.6 0.6 copy.22
Async XLA Ops:
  3.3 1.4 %copy-start = (bf16[1,1,640,1152]{3,2,1,0:T(8,128)(2,1)S(1)}, bf16[1,1,640,1152]{3,2,1,0:T(8,128)(2,1)}, u32[]{:S(2)}) copy-start(bf16[1,1,640,1152]{3,2,1,0:T(8,128)(2,1)} %param.11) | copy-start | bytes 4423684
  4.6 0.9 %copy-start.1 = (bf16[36,2152]{1,0:T(8,128)(2,1)S(1)}, bf16[36,2152]{1,0:T(8,128)(2,1)}, u32[]{:S(2)}) copy-start(bf16[36,2152]{1,0:T(8,128)(2,1)} %w1_ref.1) | copy-start | bytes 464836
  5.6 0.9 %copy-start.2 = (bf16[2152,36]{0,1:T(8,128)(2,1)S(1)}, bf16[2152,36]{0,1:T(8,128)(2,1)}, u32[]{:S(2)}) copy-start(bf16[2152,36]{0,1:T(8,128)(2,1)} %param.16) | copy-start | bytes 464836
  6.5 0.7 copy-start.3
  7.2 0.7 copy-start.4
  7.9 0.7 copy-start.5
  8.6 0.7 copy-start.6

commit v2 on v1

v2 whole, which is shorter than its diff:
```python
import jax
import jax.numpy as jnp
from jax import lax
from jax.experimental import pallas as pl
from jax.experimental.pallas import tpu as pltpu
from jax.sharding import PartitionSpec as P

MESH = pl.DeviceIdType.MESH
F32 = jnp.float32
BF16 = jnp.bfloat16
D = 1152
ROWS = 640
PIECE = 36
SET = 4 * PIECE
LANES = 128
HOPS = (1, -1, 2)
SIDES = (1, -1)
PASSED = ((0, 1), (1, 1), (-1, -1), (2, -1))
NT = (((1,), (1,)), ((), ()))


def column_origin(shape):
    r = lax.broadcasted_iota(jnp.int32, shape, 1)
    group = (r * 29128) >> 22
    inside = r - group * SET
    k = (inside * 1821) >> 16
    return r + ((group & 1) * 16 + 4 * k + (group >> 1) - group * 4 - k) * PIECE


def gelu(u):
    return 0.5 * u * (1.0 + jnp.tanh(0.7978845608028654 * (u + 0.044715 * (u * u * u))))


def two_bands(values):
    return jnp.concatenate([values[:, :640], values[:, 640:]], axis=0).astype(BF16)


def kernel(
    x_hbm,
    count_ref,
    slot_hbm,
    gain_hbm,
    w1_hbm,
    w2_hbm,
    text_hbm,
    ids_hbm,
    mult_ref,
    shift_ref,
    features_out,
    image_out,
    text_out,
    x_ref,
    slot_ref,
    gain_ref,
    w1_ref,
    w2_ref,
    text_ref,
    ids_ref,
    pieces,
    w1,
    w2,
    perm,
    normed,
    member,
    half_texts,
    texts,
    units,
    pooled,
    window,
    partial,
    returned,
    load_sem,
    send_sem,
    recv_sem,
):
    loads = [
        pltpu.make_async_copy(src, dst, load_sem.at[n])
        for n, (src, dst) in enumerate(
            [
                (w1_hbm, w1_ref),
                (w2_hbm, w2_ref),
                (text_hbm, text_ref),
                (ids_hbm, ids_ref),
                (slot_hbm, slot_ref),
                (gain_hbm, gain_ref),
                (x_hbm, x_ref),
            ]
        )
    ]
    for load in loads:
        load.start()
    blk, dp, mp = lax.axis_index("blk"), lax.axis_index("dp"), lax.axis_index("mp")
    y, c = lax.div(blk, 2), lax.rem(blk, 2)
    xl, z = lax.div(dp, 16), lax.rem(dp, 16)
    rho, k0 = lax.rem(z, 4), lax.div(z, 4)

    def dev(dy=0, dz=0, yy=None, cc=None, xx=None, mm=None):
        yy = lax.rem(y + dy + 8, 4) if yy is None else yy
        zz = lax.rem(z + dz + 32, 16)
        cc = c if cc is None else cc
        xx = xl if xx is None else xx
        mm = mp if mm is None else mm
        return {"blk": yy * 2 + cc, "dp": xx * 16 + zz, "mp": mm}

    def u_dev(off):
        return dev(dy=off * c, dz=off * (1 - c))

    def v_dev(off):
        return dev(dy=off * (1 - c), dz=off * c)

    started = []
    channels = [0]

    def send(src, dst, where, when=None):
        ch = channels[0]
        channels[0] += 1
        copy = pltpu.make_async_remote_copy(
            src_ref=src,
            dst_ref=dst,
            send_sem=send_sem.at[ch],
            recv_sem=recv_sem.at[ch],
            device_id=where,
            device_id_type=MESH,
        )
        if when is None:
            copy.start()
        else:
            pl.when(when)(copy.start)
        started.append((copy, when))
        return copy

    barrier = pltpu.get_barrier_semaphore()
    peers = [dev(dz=4), dev(dz=12)]
    for dx in (0, 1):
        for dz in (-2, -1, 0, 1, 2):
            for dc, dm in ((0, 0), (0, 1), (1, 0)):
                if (dx, dz, dc, dm) != (0, 0, 0, 0):
                    xx, cc, mm = lax.rem(xl + dx, 2), lax.rem(c + dc, 2), lax.rem(mp + dm, 2)
                    peers.append(dev(dz=dz, xx=xx, cc=cc, mm=mm))
    for dy in (1, 2, 3):
        for dc in (0, 1):
            peers.append(dev(dy=dy, cc=lax.rem(c + dc, 2)))
    for peer in peers:
        pl.semaphore_signal(barrier, inc=1, device_id=peer, device_id_type=MESH)

    def two_tiles(a, b):
        both = [a.astype(F32), b.astype(F32), jnp.zeros((8, LANES), F32)]
        return jnp.concatenate(both, axis=0).astype(BF16)

    def tile_of(ref, index):
        return ref[:, pl.ds(pl.multiple_of(index * LANES, LANES), LANES)]

    def odd_tile(ref):
        part = ref[:, 2048:2152].astype(F32)
        return jnp.concatenate([part, jnp.zeros((PIECE, 24), F32)], axis=1)

    is_even = c == 0
    core = dev(cc=1 - c)
    partner = dev(xx=1 - xl)

    def push(ref, where, when=None):
        return send(ref, ref, where, when)

    def first_phase(j, when=None):
        return [push(pieces.at[j, k0], dev(dz=dz), when) for dz in (4, 12)]

    def first_onward(j, copies, when=None):
        for copy in copies:
            if when is None:
                copy.wait_recv()
            else:
                pl.when(when)(copy.wait_recv)
        return [
            push(pieces.at[j, lax.rem(k0 + 3, 4), pl.ds(0, 48)], dev(dz=4), when),
            push(pieces.at[j, lax.rem(k0 + 1, 4), pl.ds(48, 32)], dev(dz=12), when),
        ]

    loads[0].wait()
    pieces[0, k0] = two_tiles(tile_of(w1_ref, c * 8 + y), tile_of(w1_ref, c * 8 + 4 + y))
    pl.semaphore_wait(barrier, len(peers))
    first0 = first_phase(0)
    loads[1].wait()
    pieces[1, k0] = two_tiles(odd_tile(w1_ref), odd_tile(w2_ref))
    pieces[2, k0] = two_tiles(tile_of(w2_ref, c * 8 + y), tile_of(w2_ref, c * 8 + 4 + y))

    chunk = 128

    def perm_step(i, _):
        rows = pl.ds(pl.multiple_of(i * chunk, chunk), chunk)
        origin = lax.broadcasted_iota(jnp.int32, (chunk, D), 0) + i * chunk
        perm[rows, :] = jnp.where(origin == column_origin((chunk, D)), 1.0, 0.0).astype(BF16)
        return 0

    lax.fori_loop(0, D // chunk, perm_step, 0)
    onward0 = first_onward(0, first0)
    first1 = first_phase(1, is_even)
    first2 = first_phase(2)
    for load in loads[2:]:
        load.wait()
    gain = gain_ref[...].reshape(1, D)
    band = 320

    def norm_step(i, _):
        rows = pl.ds(pl.multiple_of(i * band, band), band)
        values = x_ref[rows, :].astype(F32)
        center = values - jnp.mean(values, axis=1, keepdims=True)
        spread = jnp.mean(center * center, axis=1, keepdims=True)
        scaled = (center * lax.rsqrt(spread + 1e-06) * gain).astype(BF16)
        normed[c, rows, :] = jnp.dot(scaled, perm[...], preferred_element_type=F32).astype(BF16)
        return 0

    lax.fori_loop(0, ROWS // band, norm_step, 0)
    normed_send = push(normed.at[c], core)

    def rows_of(r, x=None):
        if x is None:
            return pl.ds(pl.multiple_of(r * 2 * SET, 16), 2 * SET)
        return pl.ds(pl.multiple_of((r * 2 + x) * SET, 16), SET)

    def place(a, o=0):
        yy = lax.rem(y + 8 - a * c - o * (1 - c), 4)
        rr = lax.rem(rho + 8 - a * (1 - c) - o * c, 4)
        return yy, rr

    def block(group, where, x=None):
        yy, rr = where
        return w1.at[group * 4 + yy, rows_of(rr, x)]

    def stacked(j, t):
        parts = [pieces[j, k].astype(F32)[PIECE * t : PIECE * (t + 1)] for k in range(4)]
        return jnp.concatenate(parts, axis=0).astype(BF16)

    along = {}

    def both_ways(group, a):
        ref = block(group, place(a))
        along[group, a, 1] = push(ref, v_dev(1))
        along[group, a, -1] = push(ref, v_dev(-1))

    for copy in onward0:
        copy.wait_recv()
    for t in range(2):
        w1[t * 4 + y, rows_of(rho, xl), :] = stacked(0, t)
    a1 = push(block(0, place(0), xl), partner)
    own1 = block(1, place(0), xl)
    across = {0: push(own1, partner)}
    b1 = {o: push(own1, u_dev(o)) for o in SIDES}
    onward1 = first_onward(1, first1, is_even)
    onward2 = first_onward(2, first2)

    text = text_ref[...].astype(F32)
    text = text * lax.rsqrt(jnp.sum(text * text, axis=1, keepdims=True) + 1e-06)
    diagonal = lax.broadcasted_iota(jnp.int32, (4, 4), 0) == lax.broadcasted_iota(jnp.int32, (4, 4), 1)
    ids = jnp.sum(jnp.where(diagonal, jnp.broadcast_to(ids_ref[...], (4, 4)), 0).astype(F32), axis=1, keepdims=True)
    text_rows = jnp.concatenate([text, jnp.broadcast_to(ids, (4, LANES))], axis=1)
    blank = jnp.zeros((4, D + LANES), F32)
    own_text = jnp.concatenate([text_rows, blank], axis=0)
    placed_text = jnp.where(mp == 0, own_text, jnp.concatenate([blank, text_rows], axis=0))
    half_texts[mp] = two_bands(placed_text)
    half_send = push(half_texts.at[mp], dev(mm=1 - mp))
    positions = lax.broadcasted_iota(jnp.int32, (8, ROWS), 1)
    slots = lax.broadcasted_iota(jnp.int32, (8, ROWS), 0)
    is_member = (jnp.broadcast_to(slot_ref[...], (8, ROWS)) == slots) & (positions < count_ref[0])
    own_member = jnp.where(is_member, 1.0, 0.0).astype(F32)
    member[c] = own_member
    member_send = push(member.at[c], core)
    own_sizes = jnp.maximum(jnp.sum(own_member, axis=1, keepdims=True), 1.0)

    def onward_pair(ref_at, copies, where, when=None):
        out = []
        for o in SIDES:
            if when is None:
                copies[o].wait_recv()
            else:
                pl.when(when)(copies[o].wait_recv)
            out.append(push(ref_at(o, 0 if o == 1 else 1), where(o), when))
        return out

    a1.wait_recv()
    pair = block(0, place(0))
    a2 = {o: push(pair, u_dev(o)) for o in SIDES}
    both_ways(0, 0)
    across[0].wait_recv()
    both_ways(1, 0)
    b2 = []
    for o in SIDES:
        b1[o].wait_recv()
        across[o] = push(block(1, place(o), xl), partner)
        yy, rr = place(o)
        start = (rr * 2 + xl) * SET + (0 if o == 1 else 80)
        part = w1.at[4 + yy, pl.ds(pl.multiple_of(start, 16), 80 if o == 1 else 64)]
        b2.append(push(part, u_dev(o)))
    a3 = onward_pair(lambda o, x: block(0, place(o), x), a2, u_dev)
    for o in SIDES:
        both_ways(0, o)
    for copy in onward1:
        pl.when(is_even)(copy.wait_recv)

    @pl.when(is_even)
    def _():
        w1[8, rows_of(rho, xl), :] = stacked(1, 0)
        w2[16] = stacked(1, 1)

    @pl.when(c == 1)
    def _():
        w1[8] = jnp.zeros((D, LANES), BF16)

    odd1 = push(w1.at[8, rows_of(rho, xl)], partner, is_even)
    for o in SIDES:
        across[o].wait_recv()
        both_ways(1, o)
    for copy in b2:
        copy.wait_recv()
    across[2] = push(block(1, place(2), xl), partner)
    for copy in a3:
        copy.wait_recv()
    both_ways(0, 2)
    for copy in onward2:
        copy.wait_recv()
    for t in range(2):
        w2[c * 8 + y * 2 + t] = stacked(2, t)
    own2 = w2.at[pl.ds(c * 8 + y * 2, 2)]
    pl.when(is_even)(odd1.wait_recv)
    odd2 = {o: push(w1.at[8, rows_of(rho)], dev(dz=o), is_even) for o in SIDES}
    patch_mean = jnp.dot(own_member.astype(BF16), x_ref[...], preferred_element_type=F32) / own_sizes

    def pass_on(group, a, o):
        along[group, a, o].wait_recv()
        along[group, a, 2 * o] = push(block(group, place(a, o)), v_dev(o))

    pass_on(0, *PASSED[0])
    pass_on(1, *PASSED[0])
    across[2].wait_recv()
    both_ways(1, 2)
    w2_sides = {o: push(own2, dev(dy=o)) for o in SIDES}
    for a, o in PASSED[1:]:
        pass_on(0, a, o)
    odd3 = onward_pair(lambda o, x: w1.at[8, rows_of(lax.rem(rho + 4 - o, 4), x)], odd2, lambda o: dev(dz=o), is_even)
    for a, o in PASSED[1:]:
        pass_on(1, a, o)
    w2_far = onward_pair(lambda o, x: w2.at[c * 8 + lax.rem(y + 4 - o, 4) * 2 + x], w2_sides, lambda o: dev(dy=o))
    half_send.wait_recv()
    texts[blk] = half_texts[0] + half_texts[1]
    text_sides = {o: push(texts.at[blk], dev(dy=o)) for o in SIDES}
    text_sends = [push(texts.at[blk], core)]

    def text_of(dy):
        return texts.at[lax.rem(y + dy + 4, 4) * 2 + c]

    member_send.wait_recv()
    normed_send.wait_recv()
    nothing = jnp.zeros((8, ROWS), F32)
    members = [
        jnp.concatenate([member[0], nothing], axis=0).astype(BF16),
        jnp.concatenate([nothing, member[1]], axis=0).astype(BF16),
    ]
    sizes = [jnp.maximum(jnp.sum(member[q], axis=1, keepdims=True), 1.0) for q in range(2)]

    def tile_work(tiles):
        weights = jnp.concatenate([w1[t] for t in tiles], axis=1)
        sums = jnp.zeros((16, LANES * len(tiles)), F32)
        for q in range(2):
            hidden = gelu(jnp.dot(normed[q], weights, preferred_element_type=F32)).astype(BF16)
            sums = sums + jnp.dot(members[q], hidden, preferred_element_type=F32)
        return sums / jnp.concatenate(sizes, axis=0)

    for copy in [copy for key, copy in along.items() if key[0] == 0 and (key[1], key[2]) not in PASSED]:
        copy.wait_recv()
    for copy in odd3:
        pl.when(is_even)(copy.wait_recv)
    low_sums = tile_work((0, 1, 2, 3, 8))
    for copy in w2_far:
        copy.wait_recv()
    for o in SIDES:
        text_sides[o].wait_recv()
    turn = 1 - 2 * c
    text_far = push(texts.at[lax.rem(y + 4 - turn, 4) * 2 + c], dev(dy=turn))
    text_sends += [push(text_of(o), core) for o in SIDES]
    w2_core = push(w2.at[pl.ds(c * 8, 8)], core)
    w2_odd = push(w2.at[16], core, is_even)
    for copy in [copy for key, copy in along.items() if key[0] == 1 and (key[1], key[2]) not in PASSED]:
        copy.wait_recv()
    high_sums = tile_work((4, 5, 6, 7))

    both_sums = jnp.concatenate([low_sums[:, :512], high_sums, low_sums[:, 512:], jnp.zeros((16, LANES), F32)], axis=1)
    for q in range(2):
        pooled[q] = two_bands(both_sums[8 * q : 8 * q + 8])
    own_window = xl * 4
    window[own_window, c] = pooled[c]
    window_sends = []
    for n, o in enumerate((0,) + HOPS):
        for dx in (0, 1):
            for dc in (0, 1):
                if (o, dx, dc) == (0, 0, 0):
                    continue
                cc = lax.rem(c + dc, 2)
                where = dev(dz=o, xx=lax.rem(xl + dx, 2), cc=cc)
                window_sends.append(send(pooled.at[cc], window.at[own_window + n, c], where))
    text_far.wait_recv()
    text_sends.append(push(text_of(2), core))
    w2_core.wait_recv()
    pl.when(c == 1)(w2_odd.wait_recv)
    order = [yy * 2 + t for t in range(2) for yy in range(4)]
    low2 = jnp.concatenate([w2[n] for n in order] + [w2[16]], axis=1)
    high2 = jnp.concatenate([w2[8 + n] for n in order], axis=1)
    for copy in window_sends:
        copy.wait_recv()
    gathered = window[...].astype(F32)
    low1 = jnp.concatenate([gathered[:, 0, :8], gathered[:, 0, 8:, :512]], axis=2).reshape(64, D).astype(BF16)
    high1 = jnp.concatenate([gathered[:, 1, :8], gathered[:, 1, 8:, :384]], axis=2).reshape(64, 1024).astype(BF16)
    result = lax.dot_general(low1, low2, NT, preferred_element_type=F32)
    result = result + lax.dot_general(high1, high2, NT, preferred_element_type=F32)
    partial[...] = jnp.concatenate([result, jnp.zeros((64, 256 - SET), F32)], axis=1)
    my_set = mp * 8 + rho * 2 + xl
    returned_sends = []
    for n, o in enumerate((0,) + HOPS):
        for dx in (0, 1):
            xx = lax.rem(xl + dx, 2)
            rows = partial.at[pl.ds(pl.multiple_of((xx * 4 + n) * 8, 8), 8)]
            for dm in (0, 1):
                if (o, dx, dm) == (0, 0, 0):
                    continue
                where = dev(dz=-o, xx=xx, mm=lax.rem(mp + dm, 2))
                returned_sends.append(send(rows, returned.at[my_set], where))
    returned[my_set] = partial[pl.ds(pl.multiple_of(xl * 32, 8), 8), :]
    for copy in returned_sends:
        copy.wait_recv()
    sums = [returned[n] + returned[8 + n] for n in range(8)]
    columns = []
    for x in range(2):
        for zz in range(16):
            k, r = zz // 4, zz % 4
            columns.append(sums[r * 2 + x][:, PIECE * k : PIECE * (k + 1)])
    features = jnp.concatenate(columns, axis=1) + patch_mean
    features_out[...] = jnp.where(mp == 0, features[:4], features[4:])

    image_unit = features * lax.rsqrt(jnp.sum(features * features, axis=1, keepdims=True) + 1e-06)
    units[blk] = two_bands(jnp.concatenate([image_unit, jnp.zeros((8, LANES), F32)], axis=1))
    unit_sends = []
    for dy in range(4):
        for dc in (0, 1):
            if (dy, dc) != (0, 0):
                where = dev(dy=dy, cc=lax.rem(c + dc, 2))
                unit_sends.append(send(units.at[blk], units.at[blk], where))
    for copy in text_sends:
        copy.wait_recv()
    mult, shift = mult_ref[0], shift_ref[0]

    def weights_of(dots, same):
        signs = jnp.where(same, 1.0, -1.0).astype(F32)
        logits = mult * dots + shift
        return (mult * -signs * jax.nn.sigmoid(-signs * logits)).astype(BF16)

    captions = texts[...].astype(F32)
    all_text = jnp.concatenate([captions[:, :8], captions[:, 8:]], axis=2).reshape(64, D + LANES)
    id_column = all_text[:, D : D + 1]
    all_text = all_text[:, :D].astype(BF16)
    square = (64, 64)
    eye = lax.broadcasted_iota(jnp.int32, square, 0) == lax.broadcasted_iota(jnp.int32, square, 1)
    id_rows = jnp.dot(
        jnp.ones((8, 64), BF16), jnp.where(eye, id_column, 0.0).astype(BF16), preferred_element_type=F32
    )
    own_images = (lax.broadcasted_iota(jnp.int32, (8, 64), 0) + blk * 8).astype(F32)
    dots = lax.dot_general(image_unit.astype(BF16), all_text, NT, preferred_element_type=F32)
    image_weights = weights_of(dots, id_rows == own_images)
    image_grads = jnp.dot(image_weights, all_text, preferred_element_type=F32)
    image_out[...] = jnp.where(mp == 0, image_grads[:4], image_grads[4:])
    for copy in unit_sends:
        copy.wait_recv()
    bands = units[...].astype(F32)
    all_units = jnp.concatenate([bands[:, :8], bands[:, 8:, :512]], axis=2).reshape(64, D).astype(BF16)
    dots = lax.dot_general(own_text[:, :D].astype(BF16), all_units, NT, preferred_element_type=F32)
    image_ids = lax.broadcasted_iota(jnp.int32, (8, 64), 1).astype(F32)
    text_weights = weights_of(dots, own_text[:, D : D + 1] == image_ids)
    text_out[...] = jnp.dot(text_weights, all_units, preferred_element_type=F32)[:4]

    for copy, when in started:
        if when is None:
            copy.wait_send()
        else:
            pl.when(when)(copy.wait_send)


CHANNELS = 136


def per_device(x, tallies, slots, gain, w1, w2, texts, ids, mult, shift):
    vmem = pl.BlockSpec(memory_space=pltpu.VMEM)
    smem = pl.BlockSpec(memory_space=pltpu.SMEM)
    hbm = pl.BlockSpec(memory_space=pltpu.HBM)
    out = jax.ShapeDtypeStruct((4, D), F32)
    results = pl.pallas_call(
        kernel,
        out_shape=(out, out, out),
        in_specs=[hbm, smem, hbm, hbm, hbm, hbm, hbm, hbm, smem, smem],
        out_specs=(vmem, vmem, vmem),
        scratch_shapes=[
            pltpu.VMEM((ROWS, D), BF16),
            pltpu.VMEM((1, ROWS), jnp.int32),
            pltpu.VMEM((D,), F32),
            pltpu.VMEM((PIECE, 2152), BF16),
            pltpu.VMEM((PIECE, 2152), BF16),
            pltpu.VMEM((4, D), BF16),
            pltpu.VMEM((1, 4), jnp.int32),
            pltpu.VMEM((3, 4, 80, LANES), BF16),
            pltpu.VMEM((9, D, LANES), BF16),
            pltpu.VMEM((17, SET, LANES), BF16),
            pltpu.VMEM((D, D), BF16),
            pltpu.VMEM((2, ROWS, D), BF16),
            pltpu.VMEM((2, 8, ROWS), F32),
            pltpu.VMEM((2, 16, 640), BF16),
            pltpu.VMEM((8, 16, 640), BF16),
            pltpu.VMEM((8, 16, 640), BF16),
            pltpu.VMEM((2, 16, 640), BF16),
            pltpu.VMEM((8, 2, 16, 640), BF16),
            pltpu.VMEM((64, 256), F32),
            pltpu.VMEM((16, 8, 256), F32),
            pltpu.SemaphoreType.DMA((7,)),
            pltpu.SemaphoreType.DMA((CHANNELS,)),
            pltpu.SemaphoreType.DMA((CHANNELS,)),
        ],
        compiler_params=pltpu.CompilerParams(
            collective_id=0, has_side_effects=True, vmem_limit_bytes=62 << 20
        ),
        name="siglip_step",
    )(
        x[0, 0],
        tallies[0],
        slots[0],
        gain,
        w1,
        w2.T,
        texts[0],
        ids,
        mult,
        shift,
    )
    return tuple(r[None] for r in results)


def solution(mesh):
    in_specs = (
        P("dp", "blk", None, None),
        P("dp", "blk"),
        P("dp", "blk", None),
        P(),
        P("dp", "mp"),
        P("mp", "dp"),
        P("dp", ("blk", "mp"), None),
        P("dp", ("blk", "mp")),
        P(),
        P(),
    )
    out_specs = (P("dp", ("blk", "mp"), None),) * 3
    return jax.shard_map(per_device, mesh=mesh, in_specs=in_specs, out_specs=out_specs, check_vma=False)
```

time: 88.6 us -> 78.1 us (0.88)
  Pallas kernels: 77.2 us -> 71.2 us
  local copies, waits for them, and re-layouts: 8.45 us -> 3.99 us
    pallas_call x1, Pallas kernels: 77.2 us -> 71.2 us  [per_device(): pl.pallas_call(kernel, out_shape=(out, out, out), in_specs=[hbm, smem, hb...]
    unnamed x17 -> x3, local copies, waits for them, and re-layouts: 7.75 us -> 3.99 us
where the time goes in v2:
time: 78.1 us; the launch traced here: 77.8 us
  Pallas kernels  71.2 us (91%)
  local copies, waits for them, and re-layouts  3.99 us (5%)
  between operations  2.58 us (3%)
    pallas_call x1, Pallas kernels, per_device(): pl.pallas_call(kernel, out_shape=(out, out, out), in_specs=[hbm, smem, hb...  71.2 us
    unnamed x3, local copies, waits for them, and re-layouts  3.99 us

profile of v2, /device:TPU:1, one launch (start us, length us, event | category | flops | bytes accessed | tf_op | source)
XLA Modules:
  0.0 77.8 jit_solution(5100374446338828518)
XLA Ops:
  2.6 71.2 %siglip_step.1 = (f32[4,1152]{1,0:T(4,128)}, f32[4,1152]{1,0:T(4,128)}, f32[4,1152]{1,0:T(4,128)}) custom-call(bf16[640,1152]{1,0:T(8,128)(2,1)} %bitcast.9, s32[1]{0:T(128)} %bitcast.8.count_ref, s32[1,640]{1,0:T(1,128)} %bitcast.15, f32[1152]{0:T(1024)} %gain_hbm.1, bf16[36,2152]{1,0:T(8,128)(2,1)} %w1_hbm.1, bf16[36,2152]{1,0:T(8,128)(2,1)} %bitcast.10, ...), custom_call_target="tpu_custom_call" | custom-call | tf_op jit(solution)/shard_map/siglip_step/pallas_call | solution.py:492
  73.8 1.3 %copy.19 = f32[1,4,1152]{2,1,0:T(4,128)} copy(f32[1,4,1152]{2,1,0:T(4,128)} %bitcast.13) | data formatting | bytes 36864
  75.1 1.3 %copy.20 = f32[1,4,1152]{2,1,0:T(4,128)} copy(f32[1,4,1152]{2,1,0:T(4,128)} %bitcast.12) | data formatting | bytes 36864
  76.5 1.3 %copy.21 = f32[1,4,1152]{2,1,0:T(4,128)} copy(f32[1,4,1152]{2,1,0:T(4,128)} %bitcast.11) | data formatting | bytes 36864

commit v3 on v2

--- a/solution.py
+++ b/solution.py
@@ -13,7 +13,6 @@
 PIECE = 36
 SET = 4 * PIECE
 LANES = 128
-HOPS = (1, -1, 2)
 SIDES = (1, -1)
 PASSED = ((0, 1), (1, 1), (-1, -1), (2, -1))
 NT = (((1,), (1,)), ((), ()))
@@ -65,8 +64,10 @@
     half_texts,
     texts,
     units,
-    pooled,
-    window,
+    pooled_low,
+    pooled_high,
+    window_low,
+    window_high,
     partial,
     returned,
     load_sem,
@@ -87,7 +88,7 @@
             ]
         )
     ]
-    for load in loads:
+    for load in loads[:6]:
         load.start()
     blk, dp, mp = lax.axis_index("blk"), lax.axis_index("dp"), lax.axis_index("mp")
     y, c = lax.div(blk, 2), lax.rem(blk, 2)
@@ -129,6 +130,16 @@
         started.append((copy, when))
         return copy
 
+    drained = [0]
+
+    def drain(end):
+        for copy, when in started[drained[0] : end]:
+            if when is None:
+                copy.wait_send()
+            else:
+                pl.when(when)(copy.wait_send)
+        drained[0] = end
+
     barrier = pltpu.get_barrier_semaphore()
     peers = [dev(dz=4), dev(dz=12)]
     for dx in (0, 1):
@@ -175,41 +186,43 @@
             push(pieces.at[j, lax.rem(k0 + 1, 4), pl.ds(48, 32)], dev(dz=12), when),
         ]
 
+    chunk = 128
+
+    def perm_step(i, _):
+        rows = pl.ds(pl.multiple_of(i * chunk, chunk), chunk)
+        origin = lax.broadcasted_iota(jnp.int32, (chunk, D), 0) + i * chunk
+        perm[rows, :] = jnp.where(origin == column_origin((chunk, D)), 1.0, 0.0).astype(BF16)
+        return 0
+
     loads[0].wait()
+    loads[6].start()
     pieces[0, k0] = two_tiles(tile_of(w1_ref, c * 8 + y), tile_of(w1_ref, c * 8 + 4 + y))
     pl.semaphore_wait(barrier, len(peers))
     first0 = first_phase(0)
     loads[1].wait()
     pieces[1, k0] = two_tiles(odd_tile(w1_ref), odd_tile(w2_ref))
     pieces[2, k0] = two_tiles(tile_of(w2_ref, c * 8 + y), tile_of(w2_ref, c * 8 + 4 + y))
-
-    chunk = 128
-
-    def perm_step(i, _):
-        rows = pl.ds(pl.multiple_of(i * chunk, chunk), chunk)
-        origin = lax.broadcasted_iota(jnp.int32, (chunk, D), 0) + i * chunk
-        perm[rows, :] = jnp.where(origin == column_origin((chunk, D)), 1.0, 0.0).astype(BF16)
-        return 0
-
-    lax.fori_loop(0, D // chunk, perm_step, 0)
-    onward0 = first_onward(0, first0)
     first1 = first_phase(1, is_even)
     first2 = first_phase(2)
+    lax.fori_loop(0, D // chunk, perm_step, 0)
     for load in loads[2:]:
         load.wait()
     gain = gain_ref[...].reshape(1, D)
-    band = 320
-
-    def norm_step(i, _):
-        rows = pl.ds(pl.multiple_of(i * band, band), band)
+    band = ROWS // 2
+
+    def normalise(i):
+        rows = pl.ds(i * band, band)
         values = x_ref[rows, :].astype(F32)
         center = values - jnp.mean(values, axis=1, keepdims=True)
         spread = jnp.mean(center * center, axis=1, keepdims=True)
         scaled = (center * lax.rsqrt(spread + 1e-06) * gain).astype(BF16)
         normed[c, rows, :] = jnp.dot(scaled, perm[...], preferred_element_type=F32).astype(BF16)
-        return 0
-
-    lax.fori_loop(0, ROWS // band, norm_step, 0)
+
+    normalise(0)
+    onward0 = first_onward(0, first0)
+    onward1 = first_onward(1, first1, is_even)
+    onward2 = first_onward(2, first2)
+    normalise(1)
     normed_send = push(normed.at[c], core)
 
     def rows_of(r, x=None):
@@ -244,9 +257,7 @@
     a1 = push(block(0, place(0), xl), partner)
     own1 = block(1, place(0), xl)
     across = {0: push(own1, partner)}
-    b1 = {o: push(own1, u_dev(o)) for o in SIDES}
-    onward1 = first_onward(1, first1, is_even)
-    onward2 = first_onward(2, first2)
+    b1 = {o: push(own1, u_dev(o)) for o in (1, -1, -2)}
 
     text = text_ref[...].astype(F32)
     text = text * lax.rsqrt(jnp.sum(text * text, axis=1, keepdims=True) + 1e-06)
@@ -276,23 +287,61 @@
             out.append(push(ref_at(o, 0 if o == 1 else 1), where(o), when))
         return out
 
+    def onward_pair(ref_at, copies, where, when=None):
+        out = []
+        for o in SIDES:
+            if when is None:
+                copies[o].wait_recv()
+            else:
+                pl.when(when)(copies[o].wait_recv)
+            out.append(push(ref_at(o, 0 if o == 1 else 1), where(o), when))
+        return out
+
+    def pass_on(group, a, o):
+        along[group, a, o].wait_recv()
+        along[group, a, 2 * o] = push(block(group, place(a, o)), v_dev(o))
+
+    last = []
+
+    def finish(a, o):
+        last.append(push(block(1, place(a, o), xl), partner))
+
+    def onward_pair(ref_at, copies, where, when=None):
+        out = []
+        for o in SIDES:
+            if when is None:
+                copies[o].wait_recv()
+            else:
+                pl.when(when)(copies[o].wait_recv)
+            out.append(push(ref_at(o, 0 if o == 1 else 1), where(o), when))
+        return out
+
+    def pass_on(group, a, o):
+        along[group, a, o].wait_recv()
+        along[group, a, 2 * o] = push(block(group, place(a, o)), v_dev(o))
+
+    last = []
+
+    def finish(a, o):
+        last.append(push(block(1, place(a, o), xl), partner))
+
     a1.wait_recv()
     pair = block(0, place(0))
-    a2 = {o: push(pair, u_dev(o)) for o in SIDES}
+    a2 = {o: push(pair, u_dev(o)) for o in (1, -1, 2)}
     both_ways(0, 0)
     across[0].wait_recv()
     both_ways(1, 0)
-    b2 = []
     for o in SIDES:
         b1[o].wait_recv()
-        across[o] = push(block(1, place(o), xl), partner)
-        yy, rr = place(o)
-        start = (rr * 2 + xl) * SET + (0 if o == 1 else 80)
-        part = w1.at[4 + yy, pl.ds(pl.multiple_of(start, 16), 80 if o == 1 else 64)]
-        b2.append(push(part, u_dev(o)))
-    a3 = onward_pair(lambda o, x: block(0, place(o), x), a2, u_dev)
-    for o in SIDES:
-        both_ways(0, o)
+        single = block(1, place(o), xl)
+        along[1, o, 1] = push(single, v_dev(1))
+        along[1, o, -1] = push(single, v_dev(-1))
+        finish(o, 0)
+    b1[-2].wait_recv()
+    across[2] = push(block(1, place(2), xl), partner)
+    for a in (1, -1, 2):
+        a2[a].wait_recv()
+        both_ways(0, a)
     for copy in onward1:
         pl.when(is_even)(copy.wait_recv)
 
@@ -306,46 +355,31 @@
         w1[8] = jnp.zeros((D, LANES), BF16)
 
     odd1 = push(w1.at[8, rows_of(rho, xl)], partner, is_even)
-    for o in SIDES:
-        across[o].wait_recv()
-        both_ways(1, o)
-    for copy in b2:
-        copy.wait_recv()
-    across[2] = push(block(1, place(2), xl), partner)
-    for copy in a3:
-        copy.wait_recv()
-    both_ways(0, 2)
+    pass_on(0, *PASSED[0])
+    pass_on(1, *PASSED[0])
+    for a in SIDES:
+        for o in SIDES:
+            along[1, a, o].wait_recv()
+            if a == o:
+                along[1, a, 2 * o] = push(block(1, place(a, o), xl), v_dev(o))
+            finish(a, o)
+    pl.when(is_even)(odd1.wait_recv)
+    odd2 = {o: push(w1.at[8, rows_of(rho)], dev(dz=o), is_even) for o in SIDES}
+    across[2].wait_recv()
+    both_ways(1, 2)
+    for a, o in PASSED[1:]:
+        pass_on(0, a, o)
     for copy in onward2:
         copy.wait_recv()
     for t in range(2):
         w2[c * 8 + y * 2 + t] = stacked(2, t)
     own2 = w2.at[pl.ds(c * 8 + y * 2, 2)]
-    pl.when(is_even)(odd1.wait_recv)
-    odd2 = {o: push(w1.at[8, rows_of(rho)], dev(dz=o), is_even) for o in SIDES}
-    patch_mean = jnp.dot(own_member.astype(BF16), x_ref[...], preferred_element_type=F32) / own_sizes
-
-    def pass_on(group, a, o):
-        along[group, a, o].wait_recv()
-        along[group, a, 2 * o] = push(block(group, place(a, o)), v_dev(o))
-
-    pass_on(0, *PASSED[0])
-    pass_on(1, *PASSED[0])
-    across[2].wait_recv()
-    both_ways(1, 2)
     w2_sides = {o: push(own2, dev(dy=o)) for o in SIDES}
-    for a, o in PASSED[1:]:
-        pass_on(0, a, o)
     odd3 = onward_pair(lambda o, x: w1.at[8, rows_of(lax.rem(rho + 4 - o, 4), x)], odd2, lambda o: dev(dz=o), is_even)
-    for a, o in PASSED[1:]:
-        pass_on(1, a, o)
-    w2_far = onward_pair(lambda o, x: w2.at[c * 8 + lax.rem(y + 4 - o, 4) * 2 + x], w2_sides, lambda o: dev(dy=o))
-    half_send.wait_recv()
-    texts[blk] = half_texts[0] + half_texts[1]
-    text_sides = {o: push(texts.at[blk], dev(dy=o)) for o in SIDES}
-    text_sends = [push(texts.at[blk], core)]
-
-    def text_of(dy):
-        return texts.at[lax.rem(y + dy + 4, 4) * 2 + c]
+    pass_on(1, *PASSED[3])
+    for a in SIDES:
+        along[1, a, 2 * a].wait_recv()
+        finish(a, 2 * a)
 
     member_send.wait_recv()
     normed_send.wait_recv()
@@ -364,65 +398,102 @@
             sums = sums + jnp.dot(members[q], hidden, preferred_element_type=F32)
         return sums / jnp.concatenate(sizes, axis=0)
 
-    for copy in [copy for key, copy in along.items() if key[0] == 0 and (key[1], key[2]) not in PASSED]:
-        copy.wait_recv()
+    own_window = xl * 4
+
+    def reach(n, cc):
+        return (0, 1, -1)[n] if n < 3 else 2 - 4 * cc
+
+    def window_phase(sums, bands, pool, there):
+        for q in range(2):
+            own = sums[8 * q : 8 * q + 8]
+            pool[q] = jnp.concatenate([own[:, :bands], own[:, bands:]], axis=0).astype(BF16)
+        there[own_window, c] = pool[c]
+        out = []
+        for n in (3, 1, 2, 0):
+            for dx in (0, 1):
+                for dc in (0, 1):
+                    if (n, dx, dc) == (0, 0, 0):
+                        continue
+                    cc = lax.rem(c + dc, 2)
+                    where = dev(dz=reach(n, cc), xx=lax.rem(xl + dx, 2), cc=cc)
+                    out.append(send(pool.at[cc], there.at[own_window + n, c], where))
+        return out
+
+    for key, copy in along.items():
+        if key[0] == 0 and key[1:] not in PASSED:
+            copy.wait_recv()
+    low_sums = tile_work((0, 1, 2, 3))
+    low_sends = window_phase(low_sums, 256, pooled_low, window_low)
+    w2_far = onward_pair(lambda o, x: w2.at[c * 8 + lax.rem(y + 4 - o, 4) * 2 + x], w2_sides, lambda o: dev(dy=o))
+    half_send.wait_recv()
+    texts[blk] = half_texts[0] + half_texts[1]
+    text_sides = {o: push(texts.at[blk], dev(dy=o)) for o in SIDES}
+    text_sends = [push(texts.at[blk], core)]
+    for copy in last:
+        copy.wait_recv()
+    for key, copy in along.items():
+        if key[0] == 1 and key[1:] not in PASSED and (key[1] in (0, 2)):
+            copy.wait_recv()
     for copy in odd3:
         pl.when(is_even)(copy.wait_recv)
-    low_sums = tile_work((0, 1, 2, 3, 8))
-    for copy in w2_far:
-        copy.wait_recv()
+    high_sums = tile_work((4, 5, 6, 7, 8))
+    high_sums = jnp.concatenate([high_sums, jnp.zeros((16, LANES), F32)], axis=1)
+    before_window = len(started)
+    high_sends = window_phase(high_sums, 384, pooled_high, window_high)
+    patch_mean = jnp.dot(own_member.astype(BF16), x_ref[...], preferred_element_type=F32) / own_sizes
     for o in SIDES:
         text_sides[o].wait_recv()
     turn = 1 - 2 * c
     text_far = push(texts.at[lax.rem(y + 4 - turn, 4) * 2 + c], dev(dy=turn))
+
+    def text_of(dy):
+        return texts.at[lax.rem(y + dy + 4, 4) * 2 + c]
+
     text_sends += [push(text_of(o), core) for o in SIDES]
+    for copy in w2_far:
+        copy.wait_recv()
     w2_core = push(w2.at[pl.ds(c * 8, 8)], core)
     w2_odd = push(w2.at[16], core, is_even)
-    for copy in [copy for key, copy in along.items() if key[0] == 1 and (key[1], key[2]) not in PASSED]:
-        copy.wait_recv()
-    high_sums = tile_work((4, 5, 6, 7))
-
-    both_sums = jnp.concatenate([low_sums[:, :512], high_sums, low_sums[:, 512:], jnp.zeros((16, LANES), F32)], axis=1)
-    for q in range(2):
-        pooled[q] = two_bands(both_sums[8 * q : 8 * q + 8])
-    own_window = xl * 4
-    window[own_window, c] = pooled[c]
-    window_sends = []
-    for n, o in enumerate((0,) + HOPS):
-        for dx in (0, 1):
-            for dc in (0, 1):
-                if (o, dx, dc) == (0, 0, 0):
-                    continue
-                cc = lax.rem(c + dc, 2)
-                where = dev(dz=o, xx=lax.rem(xl + dx, 2), cc=cc)
-                window_sends.append(send(pooled.at[cc], window.at[own_window + n, c], where))
-    text_far.wait_recv()
-    text_sends.append(push(text_of(2), core))
     w2_core.wait_recv()
     pl.when(c == 1)(w2_odd.wait_recv)
-    order = [yy * 2 + t for t in range(2) for yy in range(4)]
-    low2 = jnp.concatenate([w2[n] for n in order] + [w2[16]], axis=1)
-    high2 = jnp.concatenate([w2[8 + n] for n in order], axis=1)
-    for copy in window_sends:
-        copy.wait_recv()
-    gathered = window[...].astype(F32)
-    low1 = jnp.concatenate([gathered[:, 0, :8], gathered[:, 0, 8:, :512]], axis=2).reshape(64, D).astype(BF16)
-    high1 = jnp.concatenate([gathered[:, 1, :8], gathered[:, 1, 8:, :384]], axis=2).reshape(64, 1024).astype(BF16)
-    result = lax.dot_general(low1, low2, NT, preferred_element_type=F32)
-    result = result + lax.dot_general(high1, high2, NT, preferred_element_type=F32)
+    bands = []
+    for tiles in ((0, 1, 4, 5, 6), (2, 3, 7, 8, 9)):
+        parts = []
+        for half in range(2):
+            for n in tiles:
+                if n < 8:
+                    parts.append(w2[half * 8 + (n % 4) * 2 + n // 4])
+                elif n == 8 and half == 0:
+                    parts.append(w2[16])
+                else:
+                    parts.append(jnp.zeros((SET, LANES), BF16))
+        bands.append(jnp.concatenate(parts, axis=1))
+    drain(before_window)
+    for copy in low_sends + high_sends:
+        copy.wait_recv()
+    parts = []
+    for half in range(2):
+        parts += [window_low[:, half].reshape(128, 256), window_high[:, half].reshape(128, 384)]
+    gathered = jnp.concatenate(parts, axis=1)
+    over = [lax.dot_general(gathered, band, NT, preferred_element_type=F32).reshape(8, 16, SET) for band in bands]
+    result = (over[0][:, :8] + over[1][:, 8:]).reshape(64, SET)
     partial[...] = jnp.concatenate([result, jnp.zeros((64, 256 - SET), F32)], axis=1)
+    before_returned = len(started)
     my_set = mp * 8 + rho * 2 + xl
     returned_sends = []
-    for n, o in enumerate((0,) + HOPS):
+    for n in (3, 1, 2, 0):
         for dx in (0, 1):
             xx = lax.rem(xl + dx, 2)
             rows = partial.at[pl.ds(pl.multiple_of((xx * 4 + n) * 8, 8), 8)]
             for dm in (0, 1):
-                if (o, dx, dm) == (0, 0, 0):
+                if (n, dx, dm) == (0, 0, 0):
                     continue
-                where = dev(dz=-o, xx=xx, mm=lax.rem(mp + dm, 2))
+                where = dev(dz=-reach(n, c), xx=xx, mm=lax.rem(mp + dm, 2))
                 returned_sends.append(send(rows, returned.at[my_set], where))
     returned[my_set] = partial[pl.ds(pl.multiple_of(xl * 32, 8), 8), :]
+    text_far.wait_recv()
+    text_sends.append(push(text_of(2), core))
+    drain(before_returned)
     for copy in returned_sends:
         copy.wait_recv()
     sums = [returned[n] + returned[8 + n] for n in range(8)]
@@ -436,9 +507,10 @@
 
     image_unit = features * lax.rsqrt(jnp.sum(features * features, axis=1, keepdims=True) + 1e-06)
     units[blk] = two_bands(jnp.concatenate([image_unit, jnp.zeros((8, LANES), F32)], axis=1))
+    before_units = len(started)
     unit_sends = []
-    for dy in range(4):
-        for dc in (0, 1):
+    for dy in (2, 1, 3, 0):
+        for dc in (1, 0):
             if (dy, dc) != (0, 0):
                 where = dev(dy=dy, cc=lax.rem(c + dc, 2))
                 unit_sends.append(send(units.at[blk], units.at[blk], where))
@@ -465,6 +537,7 @@
     image_weights = weights_of(dots, id_rows == own_images)
     image_grads = jnp.dot(image_weights, all_text, preferred_element_type=F32)
     image_out[...] = jnp.where(mp == 0, image_grads[:4], image_grads[4:])
+    drain(before_units)
     for copy in unit_sends:
         copy.wait_recv()
     bands = units[...].astype(F32)
@@ -474,14 +547,18 @@
     text_weights = weights_of(dots, own_text[:, D : D + 1] == image_ids)
     text_out[...] = jnp.dot(text_weights, all_units, preferred_element_type=F32)[:4]
 
-    for copy, when in started:
-        if when is None:
-            copy.wait_send()
-        else:
-            pl.when(when)(copy.wait_send)
-
-
-CHANNELS = 136
+    drain(len(started))
+
+
+CHANNELS = 160
+
+
+def settle(*refs):
+    copies = [pltpu.make_async_copy(refs[n], refs[3 + n], refs[6].at[n]) for n in range(3)]
+    for copy in copies:
+        copy.start()
+    for copy in copies:
+        copy.wait()
 
 
 def per_device(x, tallies, slots, gain, w1, w2, texts, ids, mult, shift):
@@ -511,8 +588,10 @@
             pltpu.VMEM((2, 16, 640), BF16),
             pltpu.VMEM((8, 16, 640), BF16),
             pltpu.VMEM((8, 16, 640), BF16),
-            pltpu.VMEM((2, 16, 640), BF16),
-            pltpu.VMEM((8, 2, 16, 640), BF16),
+            pltpu.VMEM((2, 16, 256), BF16),
+            pltpu.VMEM((2, 16, 384), BF16),
+            pltpu.VMEM((8, 2, 16, 256), BF16),
+            pltpu.VMEM((8, 2, 16, 384), BF16),
             pltpu.VMEM((64, 256), F32),
             pltpu.VMEM((16, 8, 256), F32),
             pltpu.SemaphoreType.DMA((7,)),
@@ -535,6 +614,15 @@
         mult,
         shift,
     )
+    results = pl.pallas_call(
+        settle,
+        out_shape=(out, out, out),
+        in_specs=[hbm] * 3,
+        out_specs=(hbm,) * 3,
+        scratch_shapes=[pltpu.SemaphoreType.DMA((3,))],
+        compiler_params=pltpu.CompilerParams(vmem_limit_bytes=62 << 20),
+        name="settle",
+    )(*results)
     return tuple(r[None] for r in results)
 
 

time: 78.1 us -> 75.7 us (0.969)
  local copies, waits for them, and re-layouts: 3.99 us -> 0 us
  Pallas kernels: 71.2 us -> 72.9 us
    unnamed x3 -> x0, local copies, waits for them, and re-layouts: 3.99 us -> none
    pallas_call x0 -> x1, Pallas kernels: none -> 2.81 us  [per_device(): pl.pallas_call(settle, out_shape=(out, out, out), in_specs=[hbm] * 3, out...]
    pallas_call x1, Pallas kernels: 71.2 us -> 70.1 us  [per_device(): pl.pallas_call(kernel, out_shape=(out, out, out), in_specs=[hbm, smem, hb...]
where the time goes in v3:
time: 75.7 us; the launch traced here: 75.5 us
  Pallas kernels  72.9 us (96%)
  between operations  2.58 us (3%)
    pallas_call x1, Pallas kernels, per_device(): pl.pallas_call(kernel, out_shape=(out, out, out), in_specs=[hbm, smem, hb...  70.1 us
    pallas_call x1, Pallas kernels, per_device(): pl.pallas_call(settle, out_shape=(out, out, out), in_specs=[hbm] * 3, out...  2.81 us

profile of v3, /device:TPU:1, one launch (start us, length us, event | category | flops | bytes accessed | tf_op | source)
XLA Modules:
  0.0 75.5 jit_solution(18281522342424273356)
XLA Ops:
  2.6 70.1 %siglip_step.1 = (f32[4,1152]{1,0:T(4,128)}, f32[4,1152]{1,0:T(4,128)}, f32[4,1152]{1,0:T(4,128)}) custom-call(bf16[640,1152]{1,0:T(8,128)(2,1)} %bitcast.9, s32[1]{0:T(128)} %bitcast.8.count_ref, s32[1,640]{1,0:T(1,128)} %bitcast.12, f32[1152]{0:T(1024)} %gain_hbm.1, bf16[36,2152]{1,0:T(8,128)(2,1)} %w1_hbm.1, bf16[36,2152]{1,0:T(8,128)(2,1)} %bitcast.10, ...), custom_call_target="tpu_custom_call" | custom-call | tf_op jit(solution)/shard_map/siglip_step/pallas_call | solution.py:569
  72.7 2.8 %settle.1 = (f32[4,1152]{1,0:T(4,128)}, f32[4,1152]{1,0:T(4,128)}, f32[4,1152]{1,0:T(4,128)}) custom-call(f32[4,1152]{1,0:T(4,128)} %get-tuple-element.9.refs_0_, f32[4,1152]{1,0:T(4,128)} %get-tuple-element.10.refs_1_, f32[4,1152]{1,0:T(4,128)} %get-tuple-element.11.refs_2_), custom_call_target="tpu_custom_call" | custom-call | tf_op jit(solution)/shard_map/settle/pallas_call | solution.py:617

commit v4 on v3

--- a/solution.py
+++ b/solution.py
@@ -554,11 +554,8 @@
 
 
 def settle(*refs):
-    copies = [pltpu.make_async_copy(refs[n], refs[3 + n], refs[6].at[n]) for n in range(3)]
-    for copy in copies:
-        copy.start()
-    for copy in copies:
-        copy.wait()
+    for n in range(3):
+        refs[3 + n][...] = refs[n][...]
 
 
 def per_device(x, tallies, slots, gain, w1, w2, texts, ids, mult, shift):
@@ -617,9 +614,8 @@
     results = pl.pallas_call(
         settle,
         out_shape=(out, out, out),
-        in_specs=[hbm] * 3,
-        out_specs=(hbm,) * 3,
-        scratch_shapes=[pltpu.SemaphoreType.DMA((3,))],
+        in_specs=[vmem] * 3,
+        out_specs=(vmem,) * 3,
         compiler_params=pltpu.CompilerParams(vmem_limit_bytes=62 << 20),
         name="settle",
     )(*results)

time: 75.7 us -> 74.3 us (0.982)
  Pallas kernels: 72.9 us -> 71.5 us
    pallas_call x1, Pallas kernels: 2.81 us -> 1.38 us  [per_device(): pl.pallas_call(settle, out_shape=(out, out, out), in_specs=[vmem] * 3, ou...]
where the time goes in v4:
time: 74.3 us; the launch traced here: 74.1 us
  Pallas kernels  71.5 us (96%)
  between operations  2.58 us (3%)
    pallas_call x1, Pallas kernels, per_device(): pl.pallas_call(kernel, out_shape=(out, out, out), in_specs=[hbm, smem, hb...  70.1 us

profile of v4, /device:TPU:1, one launch (start us, length us, event | category | flops | bytes accessed | tf_op | source)
XLA Modules:
  0.0 74.1 jit_solution(6500614132931507146)
XLA Ops:
  2.6 70.1 %siglip_step.1 = (f32[4,1152]{1,0:T(4,128)}, f32[4,1152]{1,0:T(4,128)}, f32[4,1152]{1,0:T(4,128)}) custom-call(bf16[640,1152]{1,0:T(8,128)(2,1)} %bitcast.9, s32[1]{0:T(128)} %bitcast.8.count_ref, s32[1,640]{1,0:T(1,128)} %bitcast.12, f32[1152]{0:T(1024)} %gain_hbm.1, bf16[36,2152]{1,0:T(8,128)(2,1)} %w1_hbm.1, bf16[36,2152]{1,0:T(8,128)(2,1)} %bitcast.10, ...), custom_call_target="tpu_custom_call" | custom-call | tf_op jit(solution)/shard_map/siglip_step/pallas_call | solution.py:566
  72.7 1.4 %settle.1 = (f32[4,1152]{1,0:T(4,128)}, f32[4,1152]{1,0:T(4,128)}, f32[4,1152]{1,0:T(4,128)}) custom-call(f32[4,1152]{1,0:T(4,128)} %get-tuple-element.9.refs_0_, f32[4,1152]{1,0:T(4,128)} %get-tuple-element.10.refs_1_, f32[4,1152]{1,0:T(4,128)} %get-tuple-element.11.refs_2_), custom_call_target="tpu_custom_call" | custom-call | tf_op jit(solution)/shard_map/settle/pallas_call | solution.py:614
